TPU v7x, 512 devices: a whole 4x4x16 slice. The times are simulated.
512 devices in a mesh: zone: 32 (over z, x_hi), freq: 16 (over x_lo, y, core).
Axes of the slice: x: 4 (x_hi: 2, x_lo: 2; x = x_hi * 2 + x_lo), y: 4, z: 16, core: 2. Of those that a mesh axis runs over, the one named last changes fastest.
Arguments:
- modulus: float32 [256, 3, 1, 1024], P('zone'), may hold values from 0.3 to 1.5
- first_moment: float32 [256, 3, 1, 1024], P('zone'), may hold values from -6 to 6
- second_moment: float32 [256, 3, 1, 1024], P('zone'), may hold values from 0.5 to 4
- fiber: float32 [256, 1, 1024], P('zone'), may hold values from -1 to 1
- measured: float32 [16, 128, 2, 8, 1024], P('freq', 'zone'), may hold values from -6 to 6
- wave_sq: float32 [16], P('freq'), may hold values from 0.5 to 5
- send_list: int32 [32, 32, 2], P('zone'), may hold values from -1 to 7, as said below
- brick_list: int32 [128, 8], P('zone'), may hold values from 0 to 63, as said below
Outputs:
- new_modulus: float32 [256, 3, 1, 1024], P('zone')
- new_first: float32 [256, 3, 1, 1024], P('zone')
- new_second: float32 [256, 3, 1, 1024], P('zone')
Inputs may be any that keep to these rules, and one draw needn't show every extreme that they name: `send_list`: entries are -1 or distinct local brick indices; for each owner and zone group the live slots are c < some count of 0 to 2, and owner o sends 2 bricks to group (o + 1) % 32. `brick_list`: every entry names a live slot of its zone group.
All inputs are finite; a program needn't handle non-finite values.
Results may differ from a plain program's by a relative error of at most 0.0001.
Values sent between devices are 32-bit elements; how exact they have to be, the bound alone decides.
A program may use at most 64 MiB of HBM per device.

v0:
```python
import jax
import jax.numpy as jnp
from jax import lax
from jax.sharding import PartitionSpec as P

BY = 32
BZ = 32
K = 8
SWEEPS = 6


relax_rate = 0.25
learn_rate = 0.1
beta_first = 0.9
beta_second = 0.99
smooth_rate = 0.5
adam_eps = 1e-08


def beside_sum(cube):
    padded = jnp.pad(cube, ((0, 0), (1, 1), (1, 1), (1, 1)))
    total = padded[:, 2:, 1:-1, 1:-1] + padded[:, :-2, 1:-1, 1:-1]
    total = total + padded[:, 1:-1, 2:, 1:-1] + padded[:, 1:-1, :-2, 1:-1]
    return total + padded[:, 1:-1, 1:-1, 2:] + padded[:, 1:-1, 1:-1, :-2]


def misfit(moduli, fiber_tile, observed, wave_value):
    shear = (moduli[0] + (moduli[1] - moduli[0]) * fiber_tile * fiber_tile).reshape(-1, BY, BZ)
    damping = moduli[2].reshape(-1, BY, BZ)
    diagonal_term = 6.0 * shear + wave_value
    start_field = observed.reshape(2, -1, BY, BZ)
    field = start_field
    for sweep_index in range(SWEEPS):
        stencil = 6.0 * field - beside_sum(field)
        resid_real = shear * (stencil[0] - damping * stencil[1]) - wave_value * field[0]
        resid_imag = shear * (stencil[1] + damping * stencil[0]) - wave_value * field[1]
        field = field - relax_rate * jnp.stack([resid_real, resid_imag]) / diagonal_term
    gap = field - start_field
    return jnp.sum(gap * gap)


def update(moduli, first_moment, second_moment, fiber_tile, descent):
    new_first = beta_first * first_moment + (1.0 - beta_first) * descent
    new_second = beta_second * second_moment + (1.0 - beta_second) * descent * descent
    stepped = moduli - learn_rate * new_first / (jnp.sqrt(new_second) + adam_eps)
    shaped = stepped.reshape(stepped.shape[:-1] + (-1, BZ))
    lower_cell = jnp.concatenate([shaped[..., :1], shaped[..., :-1]], axis=-1).reshape(
        stepped.shape
    )
    upper_cell = jnp.concatenate([shaped[..., 1:], shaped[..., -1:]], axis=-1).reshape(
        stepped.shape
    )
    weight = smooth_rate * (fiber_tile * fiber_tile)[:, None]
    smoothed = stepped + weight * (0.5 * (lower_cell + upper_cell) - stepped)
    return (smoothed, new_first, new_second)


def to_owned(returned, owner_pick):
    flattened = returned.reshape(owner_pick.shape[1], -1)
    return jnp.dot(owner_pick, flattened, precision=lax.Precision.HIGHEST)


def on_device(
    modulus, first_moment, second_moment, fiber, measured, wave_sq, send_list, brick_list
):
    zone_count = lax.axis_size("zone")
    freq_count = lax.axis_size("freq")
    owned_count = modulus.shape[0]
    rows_brick = modulus.shape[2]
    depth = modulus.shape[3]
    slot_cap = send_list.shape[2]
    owner_list = send_list[0]
    live_mask = owner_list >= 0
    safe_ids = jnp.where(live_mask, owner_list, 0)
    stacked = jnp.concatenate([modulus, fiber[:, None]], axis=1)
    outgoing = jnp.where(live_mask[:, :, None, None, None], stacked[safe_ids], 0.0)
    arrived = lax.all_to_all(outgoing, "zone", split_axis=0, concat_axis=0, tiled=True)
    slot_data = arrived.reshape(zone_count * slot_cap, 4, rows_brick, depth)
    wave_value = wave_sq[0]

    def solve(subzone_item):
        brick_ids, observed = subzone_item
        picked_rows = slot_data[brick_ids]
        subzone_par = jnp.swapaxes(picked_rows, 0, 1).reshape(4, K * rows_brick, depth)
        gradient = jax.grad(misfit)(subzone_par[:3], subzone_par[3], observed, wave_value)
        return jnp.swapaxes(gradient.reshape(3, K, rows_brick, depth), 0, 1)

    gradients = lax.map(solve, (brick_list, measured[0]))
    flattened = gradients.reshape(-1, 3 * rows_brick * depth)
    references = brick_list.reshape(-1)
    slot_iota = jnp.arange(zone_count * slot_cap, dtype=jnp.int32)
    selector = (references[None, :] == slot_iota[:, None]).astype(jnp.float32)
    slot_grad = jnp.dot(selector, flattened, precision=lax.Precision.HIGHEST)
    slot_grad = slot_grad.reshape(zone_count, slot_cap, 3, rows_brick, depth)
    use_count = jnp.sum(selector, axis=1).reshape(zone_count, slot_cap)
    owned_iota = jnp.arange(owned_count, dtype=jnp.int32)
    owner_pick = (owner_list.reshape(-1)[None, :] == owned_iota[:, None]).astype(jnp.float32)
    returned, returned_uses = (
        lax.all_to_all(slot_grad, "zone", split_axis=0, concat_axis=0, tiled=True),
        lax.all_to_all(use_count, "zone", split_axis=0, concat_axis=0, tiled=True),
    )
    owned_grad = to_owned(returned, owner_pick).reshape(owned_count, 3, rows_brick, depth)
    intersection = jnp.dot(owner_pick, returned_uses.reshape(-1), precision=lax.Precision.HIGHEST)
    grad_total = lax.psum(owned_grad, "freq")
    descent = grad_total / (freq_count * jnp.maximum(intersection, 1.0))[:, None, None, None]
    return update(modulus, first_moment, second_moment, fiber, descent)


def solution(mesh):
    placed = (
        P("zone", None, None, None),
        P("zone", None, None, None),
        P("zone", None, None, None),
        P("zone", None, None),
        P("freq", "zone", None, None, None),
        P("freq"),
        P("zone", None, None),
        P("zone", None),
    )
    return jax.shard_map(
        on_device,
        mesh=mesh,
        in_specs=placed,
        out_specs=(
            P("zone", None, None, None),
            P("zone", None, None, None),
            P("zone", None, None, None),
        ),
        check_vma=False,
    )
```

profile of v0, /device:TPU:1, one launch (start us, length us, event | category | flops | bytes accessed | tf_op | source)
XLA Modules:
  0.0 472.6 jit_solution(13486487006673301540)
XLA Ops:
  8.3 1.0 pad_maximum_fusion
  9.3 1.2 gather_fusion.1
  10.5 1.3 broadcast_select_fusion
  11.8 18.5 %all-to-all-start = ((f32[32,2,4,1,1024]{4,2,1,3,0:T(4,128)}), f32[32,2,4,1,1024]{4,2,1,3,0:T(4,128)S(1)}, u32[]{:S(2)}, u32[]{:S(2)}) async-start(f32[32,2,4,1,1024]{4,2,1,3,0:T(4,128)} %broadcast_select_fusion), calls=%async_computation | async-start | bytes 2097152 | tf_op jit(solution)/shard_map/all_to_all | solution.py:77
  32.9 50.5 %all-to-all-done = f32[32,2,4,1,1024]{4,2,1,3,0:T(4,128)S(1)} async-done(((f32[32,2,4,1,1024]{4,2,1,3,0:T(4,128)}), f32[32,2,4,1,1024]{4,2,1,3,0:T(4,128)S(1)}, u32[]{:S(2)}, u32[]{:S(2)}) %all-to-all-start) | async-done | bytes 1048608 | tf_op jit(solution)/shard_map/all_to_all | solution.py:77
  83.4 7.2 %all-to-all-start.2 = ((f32[32,1,2]{2,1,0:T(1,128)}), f32[32,1,2]{2,1,0:T(1,128)S(1)}, u32[]{:S(2)}, u32[]{:S(2)}) async-start(f32[32,1,2]{2,1,0:T(1,128)} %bitcast.32), calls=%async_computation.2 | async-start | bytes 32768 | tf_op jit(solution)/shard_map/all_to_all | solution.py:100
  90.6 189.0 %while.12 = (s32[]{:T(128)}, f32[4,8,3,1,1024]{4,1,2,3,0:T(8,128)}, s32[4,8]{1,0:T(4,128)}, f32[64,4,1,1024]{3,1,0,2:T(4,128)S(1)}, f32[4,2,8,1024]{3,2,1,0:T(8,...) while((s32[]{:T(128)}, f32[4,8,3,1,1024]{4,1,2,3,0:T(8,128)}, s32[4,8]{1,0:T(4,128)}, ...), condition=%wide.region_7.8_spmd, body=%wide.region_0.7_spmd.sunk | while | flops 7111707 | bytes 32707772 | solution.py:88
  91.4 1.4 dynamic-slice_multiply_fusion.3
  96.0 1.4 multiply_divide_fusion.4
  113.3 0.9 multiply_reduce_fusion.9
  123.0 1.4 fusion.211
  126.0 0.9 copy-done.5
  127.1 1.5 fusion.213
  128.6 1.6 unstack.190
  131.0 0.9 copy-done.3
  131.9 1.0 divide_multiply_fusion.17
  138.6 1.4 dynamic-slice_multiply_fusion.3
  143.2 1.4 multiply_divide_fusion.4
  160.5 0.9 multiply_reduce_fusion.9
  170.3 1.4 fusion.211
  173.2 0.9 copy-done.5
  174.4 1.5 fusion.213
  175.8 1.6 unstack.190
  178.2 0.9 copy-done.3
  179.1 1.0 divide_multiply_fusion.17
  185.8 1.4 dynamic-slice_multiply_fusion.3
  190.5 1.4 multiply_divide_fusion.4
  207.8 0.9 multiply_reduce_fusion.9
  217.5 1.4 fusion.211
  220.4 0.9 copy-done.5
  221.6 1.5 fusion.213
  223.1 1.6 unstack.190
  226.4 1.0 divide_multiply_fusion.17
  233.1 1.4 dynamic-slice_multiply_fusion.3
  237.7 1.4 multiply_divide_fusion.4
  255.0 0.9 multiply_reduce_fusion.9
  264.7 1.4 fusion.211
  267.7 0.9 copy-done.5
  268.8 1.5 fusion.213
  270.3 1.6 unstack.190
  273.6 1.0 divide_multiply_fusion.17
  280.3 1.5 convolution_bitcast_fusion
  281.8 1.5 copy.104
  283.3 14.0 %all-to-all-start.1 = ((f32[32,2,3,1,1024]{4,1,3,2,0:T(2,128)}), f32[32,2,3,1,1024]{4,1,3,2,0:T(2,128)S(1)}, u32[]{:S(2)}, u32[]{:S(2)}) async-start(f32[32,2,3,1,1024]{4,1,3,2,0:T(2,128)} %copy.104), calls=%async_computation.1 | async-start | bytes 1572864 | tf_op jit(solution)/shard_map/all_to_all | solution.py:99
  299.4 39.1 %all-to-all-done.1 = f32[32,2,3,1,1024]{4,1,3,2,0:T(2,128)S(1)} async-done(((f32[32,2,3,1,1024]{4,1,3,2,0:T(2,128)}), f32[32,2,3,1,1024]{4,1,3,2,0:T(2,128)S(1)}, u32[]{:S(2)}, u32[]{:S(2)}) %all-to-all-start.1) | async-done | bytes 786464 | tf_op jit(solution)/shard_map/all_to_all | solution.py:99
  339.0 1.5 convolution_bitcast_fusion.1
  340.6 120.9 %all-reduce.72.cloned.1.call-done = f32[8,3,1,1024]{3,0,1,2:T(8,128)} async-done(((f32[8,3,1,1024]{3,0,1,2:T(8,128)}), f32[8,3,1,1024]{3,0,1,2:T(8,128)}) %all-reduce.72.cloned.1.call-update) | async-done | bytes 98320 | tf_op jit(solution)/shard_map/psum | solution.py:104
  461.5 1.0 copy_subtract_fusion
  (711 shorter events, 155.0 us)
Async XLA Ops:
  7.2 1.1 copy-start.33
  11.8 71.6 %all-to-all-start = ((f32[32,2,4,1,1024]{4,2,1,3,0:T(4,128)}), f32[32,2,4,1,1024]{4,2,1,3,0:T(4,128)S(1)}, u32[]{:S(2)}, u32[]{:S(2)}) async-start(f32[32,2,4,1,1024]{4,2,1,3,0:T(4,128)} %broadcast_select_fusion), calls=%async_computation | async-start | bytes 2097152 | tf_op jit(solution)/shard_map/all_to_all | solution.py:77
  83.4 199.9 %all-to-all-start.2 = ((f32[32,1,2]{2,1,0:T(1,128)}), f32[32,1,2]{2,1,0:T(1,128)S(1)}, u32[]{:S(2)}, u32[]{:S(2)}) async-start(f32[32,1,2]{2,1,0:T(1,128)} %bitcast.32), calls=%async_computation.2 | async-start | bytes 32768 | tf_op jit(solution)/shard_map/all_to_all | solution.py:100
  90.6 4.7 copy-start.30
  94.6 1.1 copy-start.1
  125.9 0.9 copy-start.5
  130.9 0.9 copy-start.3
  130.9 1.0 copy-start.4
  131.9 1.0 copy-start.6
  133.7 1.0 copy-start
  134.9 0.9 copy-start.15
  134.9 0.9 copy-start.16
  136.6 1.3 copy-start.31
  137.9 4.7 copy-start.30
  141.9 1.1 copy-start.1
  173.1 0.9 copy-start.5
  178.2 0.9 copy-start.3
  178.2 1.0 copy-start.4
  179.1 1.0 copy-start.6
  181.0 1.0 copy-start
  182.1 0.9 copy-start.15
  182.1 0.9 copy-start.16
  183.9 1.3 copy-start.31
  185.1 4.7 copy-start.30
  189.1 1.1 copy-start.1
  220.4 0.9 copy-start.5
  225.4 0.9 copy-start.3
  225.4 1.0 copy-start.4
  226.4 1.0 copy-start.6
  228.2 1.0 copy-start
  229.3 0.9 copy-start.15
  229.3 0.9 copy-start.16
  231.1 1.3 copy-start.31
  232.4 4.7 copy-start.30
  236.3 1.1 copy-start.1
  267.6 0.9 copy-start.5
  272.6 0.9 copy-start.3
  272.6 1.0 copy-start.4
  273.6 1.0 copy-start.6
  275.4 1.0 copy-start
  276.6 0.9 copy-start.16
  278.3 1.3 copy-start.31
  283.3 14.1 %copy-start.38 = (s32[1,32,2]{1,2,0:T(2,128)S(1)}, s32[1,32,2]{1,2,0:T(2,128)}, u32[]{:S(2)}) copy-start(s32[1,32,2]{1,2,0:T(2,128)} %param.16) | copy-start | bytes 772
  283.3 55.2 %all-to-all-start.1 = ((f32[32,2,3,1,1024]{4,1,3,2,0:T(2,128)}), f32[32,2,3,1,1024]{4,1,3,2,0:T(2,128)S(1)}, u32[]{:S(2)}, u32[]{:S(2)}) async-start(f32[32,2,3,1,1024]{4,1,3,2,0:T(2,128)} %copy.104), calls=%async_computation.1 | async-start | bytes 1572864 | tf_op jit(solution)/shard_map/all_to_all | solution.py:99
  297.3 164.2 %all-reduce.72.cloned.1.call-start = ((), (), s32[]{:S(2)}) async-start(), calls=%async_computation.3 | async-start | bytes 196608 | tf_op jit(solution)/shard_map/psum | solution.py:104
  339.0 122.5 %copy-start.35 = (f32[8,3,1,1024]{3,2,1,0:T(1,128)S(1)}, f32[8,3,1,1024]{3,2,1,0:T(1,128)}, u32[]{:S(2)}) copy-start(f32[8,3,1,1024]{3,2,1,0:T(1,128)} %param.11) | copy-start | bytes 294916
  339.0 122.5 %copy-start.36 = (f32[8,3,1,1024]{3,2,1,0:T(1,128)S(1)}, f32[8,3,1,1024]{3,2,1,0:T(1,128)}, u32[]{:S(2)}) copy-start(f32[8,3,1,1024]{3,2,1,0:T(1,128)} %param.12) | copy-start | bytes 294916
  340.5 121.1 %copy-start.32 = (f32[8,3,1,1024]{3,2,1,0:T(1,128)S(1)}, f32[8,3,1,1024]{3,2,1,0:T(1,128)}, u32[]{:S(2)}) copy-start(f32[8,3,1,1024]{3,2,1,0:T(1,128)} %param.10) | copy-start | bytes 294916
  (94 other events, 77.4 us)
Sparse Core Ops, SparseCore 0:
  340.6 120.8 all-reduce.71
where the time goes:
time: 476 us; the launch traced here: 473 us
  waiting for transfers between devices  211 us (44%)
  local copies, waits for them, and re-layouts  114 us (24%)
  other arithmetic  89.2 us (19%)
  starting transfers between devices  39.7 us (8%)
  between operations  14.2 us (3%)
    psum x1, waiting for transfers between devices, on_device(): grad_total = lax.psum(owned_grad, 'freq')  121 us
    all_to_all x1, waiting for transfers between devices, on_device(): lax.all_to_all(outgoing, 'zone', split_axis=0, concat_axis=0, tiled=True)  50.5 us
    all_to_all x1, waiting for transfers between devices, on_device(): lax.all_to_all(slot_grad, 'zone', split_axis=0, concat_axis=0, tiled=True)  39.1 us
    another operation x100, local copies, waits for them, and re-layouts, misfit(): jnp.stack([resid_real, resid_imag])  38.8 us
    another operation x20, other arithmetic, misfit(): jnp.stack([resid_real, resid_imag])  20.5 us
    all_to_all x1, starting transfers between devices, on_device(): lax.all_to_all(outgoing, 'zone', split_axis=0, concat_axis=0, tiled=True)  18.5 us
    squeeze x24, local copies, waits for them, and re-layouts, misfit(): stencil[0] - damping * stencil[1]  17.5 us
    squeeze x24, local copies, waits for them, and re-layouts, misfit(): stencil[1]  17.4 us
  transfers between devices with their start and end apart: 4, of which 3 were waited for; matrix products, arithmetic and copies ran while one was open for 38% of the time, Pallas kernels for 0%

commit v1 on v0

v1 whole, which is shorter than its diff:
```python
import functools

import jax
import jax.numpy as jnp
from jax import lax
from jax.experimental import pallas as pl
from jax.experimental.pallas import tpu as pltpu
from jax.sharding import PartitionSpec as P

BZ = 32
K = 8
NB = 8
SUBZ = 4
CAP = 2
YH = 8
LANES = 128
SWEEPS = 6
GROUP = 4

relax_rate = 0.25
learn_rate = 0.1
beta_first = 0.9
beta_second = 0.99
smooth_rate = 0.5
adam_eps = 1e-08

MESH = pl.DeviceIdType.MESH
HIGHEST = lax.Precision.HIGHEST


def beside_sum(x):
    lane = lax.broadcasted_iota(jnp.int32, x.shape, 3)
    sub = lax.broadcasted_iota(jnp.int32, x.shape, 2)
    z = lane % BZ
    none = jnp.zeros_like(x[:, :1])
    up = pltpu.roll(x, BZ, 3)
    up = jnp.where(lane < BZ, jnp.concatenate([none, up[:, :-1]], 1), up)
    down = pltpu.roll(x, LANES - BZ, 3)
    down = jnp.where(lane >= LANES - BZ, jnp.concatenate([down[:, 1:], none], 1), down)
    total = up + down
    total += jnp.where(z > 0, pltpu.roll(x, 1, 3), 0.0)
    total += jnp.where(z < BZ - 1, pltpu.roll(x, LANES - 1, 3), 0.0)
    total += jnp.where(sub > 0, pltpu.roll(x, 1, 2), 0.0)
    return total + jnp.where(sub < K - 1, pltpu.roll(x, K - 1, 2), 0.0)


def exchange(
    zones,
    freqs,
    group,
    mod_hbm,
    fib_hbm,
    meas_hbm,
    wave_ref,
    send_ref,
    brick_ref,
    out_ref,
    mod_v,
    fib_v,
    val_v,
    out1,
    in1,
    cnt_out,
    cnt_in,
    ent,
    in2,
    meas_v,
    wave_v,
    sten0,
    hist_v,
    hist_w,
    gsum,
    gout,
    in3,
    out4,
    in4,
    own5,
    in5,
    local_sem,
    send_sem,
    recv_sem,
):
    subs = SUBZ // group
    slots = zones * CAP
    me_z = lax.axis_index("zone")
    me_f = lax.axis_index("freq")
    plane = lax.rem(me_f, 2)
    row = lax.div(me_f, 2)
    member = lax.rem(me_f, group)
    base = me_f - member

    load_mod = pltpu.make_async_copy(mod_hbm, mod_v, local_sem.at[0])
    load_fib = pltpu.make_async_copy(fib_hbm, fib_v, local_sem.at[1])
    load_meas = pltpu.make_async_copy(
        meas_hbm.at[pl.ds(member * subs, subs)], meas_v.at[member], local_sem.at[2]
    )
    load_mod.start()
    load_fib.start()
    load_meas.start()

    barrier = pltpu.get_barrier_semaphore()

    def greet_z(i, c):
        pl.semaphore_signal(
            barrier, inc=1, device_id=(lax.rem(me_z + i, zones), me_f), device_id_type=MESH
        )
        return c

    def greet_f(i, c):
        pl.semaphore_signal(
            barrier, inc=1, device_id=(me_z, lax.rem(me_f + i, freqs)), device_id_type=MESH
        )
        return c

    lax.fori_loop(1, zones, greet_z, 0)
    lax.fori_loop(1, freqs, greet_f, 0)

    load_mod.wait()
    load_fib.wait()
    first = mod_v[pl.ds(row, NB, stride=3 * YH), :]
    second = mod_v[pl.ds(YH + row, NB, stride=3 * YH), :]
    damp = mod_v[pl.ds(2 * YH + row, NB, stride=3 * YH), :]
    fibre = fib_v[pl.ds(row, NB, stride=YH), :]
    shear = first + (second - first) * fibre * fibre
    val_v[...] = jnp.where(plane == 0, shear, damp)
    for d in range(zones):
        for c in range(CAP):
            pick = jnp.maximum(send_ref[0, c, d], 0)
            out1[d * CAP + c : d * CAP + c + 1, :] = val_v[pl.ds(pick, 1), :]

    pl.semaphore_wait(barrier, zones + freqs - 2)

    def over_z(src, dst, n):
        def body(i, c):
            peer = lax.rem(me_z + i, zones)
            pltpu.make_async_remote_copy(
                src_ref=src(peer),
                dst_ref=dst,
                send_sem=send_sem.at[n],
                recv_sem=recv_sem.at[n],
                device_id=(peer, me_f),
                device_id_type=MESH,
            ).start()
            return c

        lax.fori_loop(1, zones, body, 0)

    def over_f(src, dst, n):
        def body(i, c):
            peer = lax.rem(me_f + i, freqs)
            pltpu.make_async_remote_copy(
                src_ref=src(peer),
                dst_ref=dst,
                send_sem=send_sem.at[n],
                recv_sem=recv_sem.at[n],
                device_id=(me_z, peer),
                device_id_type=MESH,
            ).start()
            return c

        lax.fori_loop(1, freqs, body, 0)

    def arrived(ref, n):
        pltpu.make_async_copy(ref, ref, recv_sem.at[n]).wait()

    def sent(ref, n):
        pltpu.make_async_copy(ref, ref, send_sem.at[n]).wait()

    mine2 = pl.ds(me_z * CAP, CAP)
    over_z(lambda p: out1.at[pl.ds(p * CAP, CAP)], in1.at[mine2], 0)
    in1[mine2, :] = out1[mine2, :]

    wave_v[member] = jnp.full((8, LANES), wave_ref[0], jnp.float32)

    def share(i, c):
        j = lax.rem(member + i, group)
        pltpu.make_async_remote_copy(
            src_ref=meas_hbm.at[pl.ds(j * subs, subs)],
            dst_ref=meas_v.at[member],
            send_sem=send_sem.at[1],
            recv_sem=recv_sem.at[1],
            device_id=(me_z, base + j),
            device_id_type=MESH,
        ).start()
        pltpu.make_async_remote_copy(
            src_ref=wave_v.at[member],
            dst_ref=wave_v.at[member],
            send_sem=send_sem.at[2],
            recv_sem=recv_sem.at[2],
            device_id=(me_z, base + j),
            device_id_type=MESH,
        ).start()
        return c

    if group > 1:
        lax.fori_loop(1, group, share, 0)

    entries = SUBZ * K
    lane_e = lax.broadcasted_iota(jnp.int32, (1, entries), 1)
    names = jnp.zeros((1, entries), jnp.int32)
    for e in range(entries):
        names = jnp.where(lane_e == e, brick_ref[e // K, e % K], names)
    named = (lax.broadcasted_iota(jnp.int32, (slots, entries), 0) == names).astype(jnp.float32)
    cnt_out[...] = jnp.broadcast_to(jnp.sum(named, 1, keepdims=True), (slots, LANES))
    over_z(lambda p: cnt_out.at[pl.ds(p * CAP, CAP)], cnt_in.at[mine2], 3)
    cnt_in[mine2, :] = cnt_out[mine2, :]

    arrived(in1.at[pl.ds(0, (zones - 1) * CAP)], 0)
    for e in range(entries):
        ent[e // K, e % K : e % K + 1, :] = in1[pl.ds(brick_ref[e // K, e % K], 1), :]
    over_f(
        lambda p: ent.at[pl.ds(lax.rem(p, group) * subs, subs)],
        in2.at[me_f],
        4,
    )
    in2[me_f] = ent[pl.ds(member * subs, subs)]

    load_meas.wait()
    if group > 1:
        arrived(meas_v.at[pl.ds(0, group - 1)], 1)
        arrived(wave_v.at[pl.ds(0, group - 1)], 2)

    def first_stencil(i, c):
        g, s = lax.div(i, subs), lax.rem(i, subs)
        sten0[i] = beside_sum(meas_v[g, s])
        return c

    lax.fori_loop(0, group * subs, first_stencil, 0)

    lane_s = lax.broadcasted_iota(jnp.int32, (1, slots), 1)
    held = jnp.zeros((1, slots), jnp.int32)
    for d in range(zones):
        for c in range(CAP):
            held = jnp.where(lane_s == d * CAP + c, send_ref[0, c, d], held)
    holds = (lax.broadcasted_iota(jnp.int32, (NB, slots), 0) == held).astype(jnp.float32)

    arrived(in2.at[pl.ds(0, freqs - 1)], 4)

    gsum[...] = jnp.zeros_like(gsum)

    def solve(i, c):
        g, s = lax.div(i, subs), lax.rem(i, subs)
        wave = wave_v[g][None]
        shear = jnp.stack([in2[2 * y, s] for y in range(YH)])
        damp = jnp.stack([in2[2 * y + 1, s] for y in range(YH)])
        inv = 1.0 / (6.0 * shear + wave)
        a = relax_rate * shear * inv
        b = a * damp
        start = meas_v[g, s]
        field = start
        near = sten0[i]
        for t in range(SWEEPS):
            if t:
                near = beside_sum(field)
            six = 6.0 * field
            w = near - six
            v = w - six
            hist_v[t] = v
            hist_w[t] = w
            real = 1.25 * field[0] + a * v[0] - b * w[1]
            imag = 1.25 * field[1] + a * v[1] + b * w[0]
            field = jnp.stack([real, imag])
        lam = 2.0 * (field - start)
        grad_a = jnp.zeros_like(a)
        grad_b = jnp.zeros_like(a)
        for t in reversed(range(SWEEPS)):
            v = hist_v[t]
            w = hist_w[t]
            grad_a += lam[0] * v[0] + lam[1] * v[1]
            grad_b += lam[1] * w[0] - lam[0] * w[1]
            if t:
                a_lam = a * lam
                push = a_lam + jnp.stack([b * lam[1], -(b * lam[0])])
                lam = 1.25 * lam - 6.0 * (push + a_lam) + beside_sum(push)
        gsum[s, 0] += (grad_a + damp * grad_b) * (relax_rate * wave * inv * inv)
        gsum[s, 1] += a * grad_b
        return c

    lax.fori_loop(0, group * subs, solve, 0)

    for s in range(subs):
        for p in range(2):
            for y in range(YH):
                gout[2 * y + p, s] = gsum[s, p, y]
    over_f(lambda p: gout.at[p], in3.at[me_f], 5)
    in3[me_f] = gout[me_f]
    arrived(in3.at[pl.ds(0, freqs - 1)], 5)
    parts = []
    for j in range(group):
        total = in3[j]
        for m in range(1, freqs // group):
            total = total + in3[m * group + j]
        parts.append(total.reshape(subs * K, LANES))
    grads = jnp.concatenate(parts, 0)
    out4[...] = jnp.dot(named, grads, precision=HIGHEST, preferred_element_type=jnp.float32)
    over_z(lambda p: out4.at[pl.ds(p * CAP, CAP)], in4.at[mine2], 6)
    in4[mine2, :] = out4[mine2, :]
    arrived(cnt_in.at[pl.ds(0, (zones - 1) * CAP)], 3)
    uses = jnp.dot(holds, cnt_in[...], precision=HIGHEST, preferred_element_type=jnp.float32)
    scale = 1.0 / (freqs * jnp.maximum(uses, 1.0))
    arrived(in4.at[pl.ds(0, (zones - 1) * CAP)], 6)
    owned = jnp.dot(holds, in4[...], precision=HIGHEST, preferred_element_type=jnp.float32)
    own5[...] = owned * scale
    mine8 = pl.ds(pl.multiple_of(me_f * NB, NB), NB)
    over_f(lambda p: own5, in5.at[mine8], 7)
    in5[mine8, :] = own5[...]
    arrived(in5.at[pl.ds(0, (freqs - 1) * NB)], 7)
    out_ref[...] = in5[...]

    sent(out1.at[pl.ds(0, (zones - 1) * CAP)], 0)
    if group > 1:
        sent(meas_v.at[pl.ds(0, group - 1)], 1)
        sent(wave_v.at[pl.ds(0, group - 1)], 2)
    sent(cnt_out.at[pl.ds(0, (zones - 1) * CAP)], 3)
    sent(in2.at[pl.ds(0, freqs - 1)], 4)
    sent(gout.at[pl.ds(0, freqs - 1)], 5)
    sent(out4.at[pl.ds(0, (zones - 1) * CAP)], 6)
    sent(in5.at[pl.ds(0, (freqs - 1) * NB)], 7)


def update(desc_ref, mod_ref, first_ref, second_ref, fib_ref, new_mod, new_first, new_second):
    lane = lax.broadcasted_iota(jnp.int32, (YH, LANES), 1)
    z = lane % BZ
    for b in range(NB):
        fibre = fib_ref[b * YH : (b + 1) * YH, :]
        square = fibre * fibre
        by_shear = desc_ref[pl.ds(b, YH, stride=2 * NB), :]
        by_damp = desc_ref[pl.ds(NB + b, YH, stride=2 * NB), :]
        by_second = by_shear * square
        for j, descent in enumerate((by_shear - by_second, by_second, by_damp)):
            at = slice((b * 3 + j) * YH, (b * 3 + j + 1) * YH)
            m1 = beta_first * first_ref[at, :] + (1.0 - beta_first) * descent
            m2 = beta_second * second_ref[at, :] + (1.0 - beta_second) * descent * descent
            stepped = mod_ref[at, :] - learn_rate * m1 / (jnp.sqrt(m2) + adam_eps)
            lower = jnp.where(z > 0, pltpu.roll(stepped, 1, 1), stepped)
            upper = jnp.where(z < BZ - 1, pltpu.roll(stepped, LANES - 1, 1), stepped)
            new_first[at, :] = m1
            new_second[at, :] = m2
            new_mod[at, :] = stepped + smooth_rate * square * (0.5 * (lower + upper) - stepped)


def on_device(
    zones, freqs, modulus, first_moment, second_moment, fiber, measured, wave_sq, send_list, brick_list
):
    group = GROUP
    subs = SUBZ // group
    slots = zones * CAP
    mod = modulus.reshape(NB * 3 * YH, LANES)
    m1 = first_moment.reshape(NB * 3 * YH, LANES)
    m2 = second_moment.reshape(NB * 3 * YH, LANES)
    fib = fiber.reshape(NB * YH, LANES)
    meas = measured.reshape(SUBZ, 2, K, YH, LANES).transpose(0, 1, 3, 2, 4)
    f32 = jnp.float32
    vmem = pltpu.VMEM
    any_spec = pl.BlockSpec(memory_space=pl.ANY)
    smem_spec = pl.BlockSpec(memory_space=pltpu.SMEM)
    vmem_spec = pl.BlockSpec(memory_space=vmem)
    plane_shape = (2, YH, K, LANES)
    descent = pl.pallas_call(
        functools.partial(exchange, zones, freqs, group),
        out_shape=jax.ShapeDtypeStruct((freqs * NB, LANES), f32),
        in_specs=[any_spec, any_spec, any_spec, smem_spec, smem_spec, smem_spec],
        out_specs=vmem_spec,
        scratch_shapes=[
            vmem((NB * 3 * YH, LANES), f32),
            vmem((NB * YH, LANES), f32),
            vmem((NB, LANES), f32),
            vmem((slots, LANES), f32),
            vmem((slots, LANES), f32),
            vmem((slots, LANES), f32),
            vmem((slots, LANES), f32),
            vmem((SUBZ, K, LANES), f32),
            vmem((freqs, subs, K, LANES), f32),
            vmem((group, subs) + plane_shape, f32),
            vmem((group, 8, LANES), f32),
            vmem((group * subs,) + plane_shape, f32),
            vmem((SWEEPS,) + plane_shape, f32),
            vmem((SWEEPS,) + plane_shape, f32),
            vmem((subs,) + plane_shape, f32),
            vmem((freqs, subs, K, LANES), f32),
            vmem((freqs, subs, K, LANES), f32),
            vmem((slots, LANES), f32),
            vmem((slots, LANES), f32),
            vmem((NB, LANES), f32),
            vmem((freqs * NB, LANES), f32),
            pltpu.SemaphoreType.DMA((3,)),
            pltpu.SemaphoreType.DMA((8,)),
            pltpu.SemaphoreType.DMA((8,)),
        ],
        compiler_params=pltpu.CompilerParams(
            collective_id=0, has_side_effects=True, vmem_limit_bytes=60 * 2**20
        ),
    )(mod, fib, meas, wave_sq, send_list.transpose(0, 2, 1), brick_list)
    made = jax.ShapeDtypeStruct((NB * 3 * YH, LANES), f32)
    outs = pl.pallas_call(
        update,
        out_shape=(made, made, made),
        in_specs=[vmem_spec] * 5,
        out_specs=(vmem_spec,) * 3,
    )(descent, mod, m1, m2, fib)
    return tuple(o.reshape(modulus.shape) for o in outs)


def solution(mesh):
    placed = (
        P("zone", None, None, None),
        P("zone", None, None, None),
        P("zone", None, None, None),
        P("zone", None, None),
        P("freq", "zone", None, None, None),
        P("freq"),
        P("zone", None, None),
        P("zone", None),
    )
    return jax.shard_map(
        functools.partial(on_device, mesh.shape["zone"], mesh.shape["freq"]),
        mesh=mesh,
        in_specs=placed,
        out_specs=(P("zone", None, None, None),) * 3,
        check_vma=False,
    )
```

time: 476 us -> 60.2 us (0.13)
  waiting for transfers between devices: 211 us -> 0 us
  local copies, waits for them, and re-layouts: 114 us -> 0 us
  other arithmetic: 89.2 us -> 0 us
  Pallas kernels: 0 us -> 58.7 us
  starting transfers between devices: 39.7 us -> 0 us
  between operations: 14.2 us -> 1.28 us
    psum x1 -> x0, waiting for transfers between devices: 121 us -> none  [on_device(): grad_total = lax.psum(owned_grad, 'freq')]
    all_to_all x3 -> x0, waiting for transfers between devices: 89.7 us -> none  [the longest x1 50.5 us: on_device(): lax.all_to_all(outgoing, 'zone', split_axis=0, concat_axis=0, tiled=True)]
    pallas_call x0 -> x2, Pallas kernels: none -> 58.7 us  [the longest x1 56.9 us: on_device(): pl.pallas_call(functools.partial(exchange, zones, freqs, group), out_shap...]
    all_to_all x3 -> x0, starting transfers between devices: 39.7 us -> none  [the longest x1 18.5 us: on_device(): lax.all_to_all(outgoing, 'zone', split_axis=0, concat_axis=0, tiled=True)]
    another operation x100 -> x0, local copies, waits for them, and re-layouts: 38.8 us -> none  [misfit(): jnp.stack([resid_real, resid_imag])]
    squeeze x80 -> x0, local copies, waits for them, and re-layouts: 37.6 us -> none  [the longest x24 17.5 us: misfit(): stencil[0] - damping * stencil[1]]
    sub x73 -> x0, other arithmetic: 23.4 us -> none  [the longest x24 14.6 us: misfit(): shear * (stencil[0] - damping * stencil[1]) - wave_value * field[0]]
    another operation x20 -> x0, other arithmetic: 20.5 us -> none  [misfit(): jnp.stack([resid_real, resid_imag])]
  transfers between devices with their start and end apart: 4 -> 0, of which waited for: 3 -> 0; matrix products, arithmetic and copies ran while one was open for 38% -> 0% of each run, Pallas kernels for 0% -> 0%
where the time goes in v1:
time: 60.2 us; the launch traced here: 60 us
  Pallas kernels  58.7 us (98%)
  between operations  1.28 us (2%)
    pallas_call x1, Pallas kernels, on_device(): pl.pallas_call(functools.partial(exchange, zones, freqs, group), out_shap...  56.9 us
    pallas_call x1, Pallas kernels, on_device(): pl.pallas_call(update, out_shape=(made, made, made), in_specs=[vmem_spec]...  1.83 us

profile of v1, /device:TPU:1, one launch (start us, length us, event | category | flops | bytes accessed | tf_op | source)
XLA Modules:
  0.0 60.0 jit_solution(11694494821519524903)
XLA Ops:
  1.3 56.9 %shard_map.103.desc_ref = f32[128,128]{1,0:T(8,128)} custom-call(f32[192,128]{1,0:T(8,128)} %bitcast.11, f32[64,128]{1,0:T(8,128)} %bitcast.14, f32[4,2,8,8,128]{4,3,2,1,0:T(8,128)} %bitcast.13, f32[1]{0:T(128)S(6)} %copy.17.wave_ref, s32[1,2,32]{2,1,0:T(2,128)} %bitcast.18, s32[4,8]{1,0:T(4,128)} %brick_ref.1), custom_call_target="tpu_custom_call" | custom-call | tf_op jit(solution)/shard_map/pallas_call | solution.py:359
  58.2 1.8 %shard_map.104 = (f32[192,128]{1,0:T(8,128)}, f32[192,128]{1,0:T(8,128)}, f32[192,128]{1,0:T(8,128)}) custom-call(f32[128,128]{1,0:T(8,128)} %shard_map.103.desc_ref, f32[192,128]{1,0:T(8,128)} %bitcast.12, f32[192,128]{1,0:T(8,128)} %bitcast.16, f32[192,128]{1,0:T(8,128)} %bitcast.17, f32[64,128]{1,0:T(8,128)} %bitcast.15), custom_call_target="tpu_custom_call" | custom-call | tf_op jit(solution)/shard_map/pallas_call | solution.py:395

commit v2 on v1

--- a/solution.py
+++ b/solution.py
@@ -15,6 +15,8 @@
 YH = 8
 LANES = 128
 SWEEPS = 6
+BY = 32
+STEP = 8
 GROUP = 4
 
 relax_rate = 0.25
@@ -28,20 +30,60 @@
 HIGHEST = lax.Precision.HIGHEST
 
 
-def beside_sum(x):
+def quarters(shape=(K, LANES)):
+    lane = lax.broadcasted_iota(jnp.int32, shape, len(shape) - 1)
+    return lane < 2 * BZ, lane % (2 * BZ) < BZ
+
+
+def turn(x, n):
+    return pltpu.roll(x, n * BZ, 1)
+
+
+def transposed(x):
+    low, even = quarters()
+    n0 = jnp.where(low, x[0], turn(x[2], 2))
+    n1 = jnp.where(low, x[1], turn(x[3], 2))
+    n2 = jnp.where(low, turn(x[0], 2), x[2])
+    n3 = jnp.where(low, turn(x[1], 2), x[3])
+    return (
+        jnp.where(even, n0, turn(n1, 1)),
+        jnp.where(even, turn(n0, 3), n1),
+        jnp.where(even, n2, turn(n3, 1)),
+        jnp.where(even, turn(n2, 3), n3),
+    )
+
+
+def spread(x):
+    low, even = quarters()
+    r = (x, turn(x, 1), turn(x, 2), turn(x, 3))
+    return tuple(
+        jnp.where(
+            low,
+            jnp.where(even, r[(-q) % 4], r[(1 - q) % 4]),
+            jnp.where(even, r[(2 - q) % 4], r[(3 - q) % 4]),
+        )
+        for q in range(4)
+    )
+
+
+def folded(x):
+    low, even = quarters()
+    p0 = jnp.where(low, x[0], x[2]) + turn(jnp.where(low, x[2], x[0]), 2)
+    p1 = jnp.where(low, x[1], x[3]) + turn(jnp.where(low, x[3], x[1]), 2)
+    rest = jnp.where(even, p1, p0)
+    return jnp.where(even, p0, p1) + jnp.where(even, turn(rest, 3), turn(rest, 1))
+
+
+def beside_sum(ref, y):
+    x = ref[:, y + 1 : y + 1 + STEP]
     lane = lax.broadcasted_iota(jnp.int32, x.shape, 3)
     sub = lax.broadcasted_iota(jnp.int32, x.shape, 2)
     z = lane % BZ
-    none = jnp.zeros_like(x[:, :1])
-    up = pltpu.roll(x, BZ, 3)
-    up = jnp.where(lane < BZ, jnp.concatenate([none, up[:, :-1]], 1), up)
-    down = pltpu.roll(x, LANES - BZ, 3)
-    down = jnp.where(lane >= LANES - BZ, jnp.concatenate([down[:, 1:], none], 1), down)
-    total = up + down
+    total = ref[:, y : y + STEP] + ref[:, y + 2 : y + 2 + STEP]
     total += jnp.where(z > 0, pltpu.roll(x, 1, 3), 0.0)
     total += jnp.where(z < BZ - 1, pltpu.roll(x, LANES - 1, 3), 0.0)
     total += jnp.where(sub > 0, pltpu.roll(x, 1, 2), 0.0)
-    return total + jnp.where(sub < K - 1, pltpu.roll(x, K - 1, 2), 0.0)
+    return x, total + jnp.where(sub < K - 1, pltpu.roll(x, K - 1, 2), 0.0)
 
 
 def exchange(
@@ -66,10 +108,16 @@
     in2,
     meas_v,
     wave_v,
-    sten0,
-    hist_v,
-    hist_w,
-    gsum,
+    field_v,
+    sten_v,
+    a_v,
+    b_v,
+    damp_v,
+    slope_v,
+    lam_v,
+    push_v,
+    by_a_v,
+    by_b_v,
     gout,
     in3,
     out4,
@@ -94,15 +142,11 @@
     load_meas = pltpu.make_async_copy(
         meas_hbm.at[pl.ds(member * subs, subs)], meas_v.at[member], local_sem.at[2]
     )
-    load_mod.start()
-    load_fib.start()
-    load_meas.start()
-
     barrier = pltpu.get_barrier_semaphore()
 
     def greet_z(i, c):
         pl.semaphore_signal(
-            barrier, inc=1, device_id=(lax.rem(me_z + i, zones), me_f), device_id_type=MESH
+            barrier, inc=1, device_id=(lax.rem(me_z + zones + zones // 2 + jnp.where(lax.rem(i, 2) == 0, lax.div(i, 2), -lax.div(i, 2)), zones), me_f), device_id_type=MESH
         )
         return c
 
@@ -114,6 +158,9 @@
 
     lax.fori_loop(1, zones, greet_z, 0)
     lax.fori_loop(1, freqs, greet_f, 0)
+    load_mod.start()
+    load_fib.start()
+    load_meas.start()
 
     load_mod.wait()
     load_fib.wait()
@@ -132,7 +179,8 @@
 
     def over_z(src, dst, n):
         def body(i, c):
-            peer = lax.rem(me_z + i, zones)
+            k = lax.div(i, 2)
+            peer = lax.rem(me_z + zones + zones // 2 + jnp.where(lax.rem(i, 2) == 0, k, -k), zones)
             pltpu.make_async_remote_copy(
                 src_ref=src(peer),
                 dst_ref=dst,
@@ -220,12 +268,24 @@
         arrived(meas_v.at[pl.ds(0, group - 1)], 1)
         arrived(wave_v.at[pl.ds(0, group - 1)], 2)
 
-    def first_stencil(i, c):
-        g, s = lax.div(i, subs), lax.rem(i, subs)
-        sten0[i] = beside_sum(meas_v[g, s])
-        return c
-
-    lax.fori_loop(0, group * subs, first_stencil, 0)
+    for t in range(SWEEPS):
+        field_v[t, :, 0] = jnp.zeros((2, K, LANES), jnp.float32)
+        field_v[t, :, BY + 1] = jnp.zeros((2, K, LANES), jnp.float32)
+    push_v[:, 0] = jnp.zeros((2, K, LANES), jnp.float32)
+    push_v[:, BY + 1] = jnp.zeros((2, K, LANES), jnp.float32)
+    for p in range(2):
+        for y in range(YH):
+            for q, tile in enumerate(transposed([meas_v[g, 0, p, y] for g in range(group)])):
+                field_v[0, p, 1 + 4 * y + q] = tile
+    low, even = quarters()
+    wave = jnp.where(
+        low,
+        jnp.where(even, wave_v[0], wave_v[1]),
+        jnp.where(even, wave_v[2], wave_v[3]),
+    )
+    for y in range(0, BY, STEP):
+        x, near = beside_sum(field_v.at[0], y)
+        sten_v[0, :, y : y + STEP] = near - 6.0 * x
 
     lane_s = lax.broadcasted_iota(jnp.int32, (1, slots), 1)
     held = jnp.zeros((1, slots), jnp.int32)
@@ -236,52 +296,68 @@
 
     arrived(in2.at[pl.ds(0, freqs - 1)], 4)
 
-    gsum[...] = jnp.zeros_like(gsum)
-
-    def solve(i, c):
-        g, s = lax.div(i, subs), lax.rem(i, subs)
-        wave = wave_v[g][None]
-        shear = jnp.stack([in2[2 * y, s] for y in range(YH)])
-        damp = jnp.stack([in2[2 * y + 1, s] for y in range(YH)])
-        inv = 1.0 / (6.0 * shear + wave)
-        a = relax_rate * shear * inv
-        b = a * damp
-        start = meas_v[g, s]
-        field = start
-        near = sten0[i]
-        for t in range(SWEEPS):
+    for y in range(YH):
+        for q, (shear, damp) in enumerate(zip(spread(in2[2 * y, 0]), spread(in2[2 * y + 1, 0]))):
+            inv = 1.0 / (6.0 * shear + wave)
+            a = relax_rate * shear * inv
+            a_v[4 * y + q] = a
+            b_v[4 * y + q] = a * damp
+            damp_v[4 * y + q] = damp
+            slope_v[4 * y + q] = relax_rate * wave * inv * inv
+
+    for t in range(SWEEPS):
+        for y in range(0, BY, STEP):
+            rows = slice(y, y + STEP)
             if t:
-                near = beside_sum(field)
-            six = 6.0 * field
-            w = near - six
+                x, near = beside_sum(field_v.at[t], y)
+                six = 6.0 * x
+                w = near - six
+                sten_v[t, :, rows] = w
+            else:
+                x = field_v[0, :, y + 1 : y + 1 + STEP]
+                six = 6.0 * x
+                w = sten_v[0, :, rows]
             v = w - six
-            hist_v[t] = v
-            hist_w[t] = w
-            real = 1.25 * field[0] + a * v[0] - b * w[1]
-            imag = 1.25 * field[1] + a * v[1] + b * w[0]
-            field = jnp.stack([real, imag])
-        lam = 2.0 * (field - start)
-        grad_a = jnp.zeros_like(a)
-        grad_b = jnp.zeros_like(a)
-        for t in reversed(range(SWEEPS)):
-            v = hist_v[t]
-            w = hist_w[t]
-            grad_a += lam[0] * v[0] + lam[1] * v[1]
-            grad_b += lam[1] * w[0] - lam[0] * w[1]
+            a, b = a_v[rows], b_v[rows]
+            real = 1.25 * x[0] + (a * v[0] - b * w[1])
+            imag = 1.25 * x[1] + (a * v[1] + b * w[0])
+            if t < SWEEPS - 1:
+                field_v[t + 1, 0, y + 1 : y + 1 + STEP] = real
+                field_v[t + 1, 1, y + 1 : y + 1 + STEP] = imag
+            else:
+                lam_v[0, rows] = 2.0 * (real - field_v[0, 0, y + 1 : y + 1 + STEP])
+                lam_v[1, rows] = 2.0 * (imag - field_v[0, 1, y + 1 : y + 1 + STEP])
+    for t in reversed(range(SWEEPS)):
+        for y in range(0, BY, STEP):
+            rows = slice(y, y + STEP)
+            lam = lam_v[:, rows]
+            w = sten_v[t, :, rows]
+            v = w - 6.0 * field_v[t, :, y + 1 : y + 1 + STEP]
+            by_a = lam[0] * v[0] + lam[1] * v[1]
+            by_b = lam[1] * w[0] - lam[0] * w[1]
+            if t < SWEEPS - 1:
+                by_a += by_a_v[rows]
+                by_b += by_b_v[rows]
+            a, b = a_v[rows], b_v[rows]
             if t:
-                a_lam = a * lam
-                push = a_lam + jnp.stack([b * lam[1], -(b * lam[0])])
-                lam = 1.25 * lam - 6.0 * (push + a_lam) + beside_sum(push)
-        gsum[s, 0] += (grad_a + damp * grad_b) * (relax_rate * wave * inv * inv)
-        gsum[s, 1] += a * grad_b
-        return c
-
-    lax.fori_loop(0, group * subs, solve, 0)
-
-    for s in range(subs):
-        for p in range(2):
-            for y in range(YH):
-                gout[2 * y + p, s] = gsum[s, p, y]
+                by_a_v[rows] = by_a
+                by_b_v[rows] = by_b
+                push_v[0, y + 1 : y + 1 + STEP] = a * lam[0] + b * lam[1]
+                push_v[1, y + 1 : y + 1 + STEP] = a * lam[1] - b * lam[0]
+            else:
+                by_shear = (by_a + damp_v[rows] * by_b) * slope_v[rows]
+                by_damp = a * by_b
+                for h in range(STEP // 4):
+                    n = y // 4 + h
+                    gout[2 * n, 0] = folded([by_shear[4 * h + q] for q in range(4)])
+                    gout[2 * n + 1, 0] = folded([by_damp[4 * h + q] for q in range(4)])
+        if t:
+            for y in range(0, BY, STEP):
+                rows = slice(y, y + STEP)
+                push, near = beside_sum(push_v, y)
+                lam = lam_v[:, rows]
+                lam_v[:, rows] = 1.25 * lam - 6.0 * (push + a_v[rows] * lam) + near
+
     over_f(lambda p: gout.at[p], in3.at[me_f], 5)
     in3[me_f] = gout[me_f]
     arrived(in3.at[pl.ds(0, freqs - 1)], 5)
@@ -373,10 +449,16 @@
             vmem((freqs, subs, K, LANES), f32),
             vmem((group, subs) + plane_shape, f32),
             vmem((group, 8, LANES), f32),
-            vmem((group * subs,) + plane_shape, f32),
-            vmem((SWEEPS,) + plane_shape, f32),
-            vmem((SWEEPS,) + plane_shape, f32),
-            vmem((subs,) + plane_shape, f32),
+            vmem((SWEEPS, 2, BY + 2, K, LANES), f32),
+            vmem((SWEEPS, 2, BY, K, LANES), f32),
+            vmem((BY, K, LANES), f32),
+            vmem((BY, K, LANES), f32),
+            vmem((BY, K, LANES), f32),
+            vmem((BY, K, LANES), f32),
+            vmem((2, BY, K, LANES), f32),
+            vmem((2, BY + 2, K, LANES), f32),
+            vmem((BY, K, LANES), f32),
+            vmem((BY, K, LANES), f32),
             vmem((freqs, subs, K, LANES), f32),
             vmem((freqs, subs, K, LANES), f32),
             vmem((slots, LANES), f32),

time: 60.2 us -> 54.7 us (0.909)
  Pallas kernels: 58.7 us -> 53.2 us
    pallas_call x1, Pallas kernels: 56.9 us -> 51.4 us  [on_device(): pl.pallas_call(functools.partial(exchange, zones, freqs, group), out_shap...]
where the time goes in v2:
time: 54.7 us; the launch traced here: 54.5 us
  Pallas kernels  53.2 us (97%)
  between operations  1.28 us (2%)
    pallas_call x1, Pallas kernels, on_device(): pl.pallas_call(functools.partial(exchange, zones, freqs, group), out_shap...  51.4 us
    pallas_call x1, Pallas kernels, on_device(): pl.pallas_call(update, out_shape=(made, made, made), in_specs=[vmem_spec]...  1.83 us

profile of v2, /device:TPU:1, one launch (start us, length us, event | category | flops | bytes accessed | tf_op | source)
XLA Modules:
  0.0 54.5 jit_solution(10096567768963846748)
XLA Ops:
  1.3 51.4 %shard_map.103.desc_ref = f32[128,128]{1,0:T(8,128)} custom-call(f32[192,128]{1,0:T(8,128)} %bitcast.11, f32[64,128]{1,0:T(8,128)} %bitcast.14, f32[4,2,8,8,128]{4,3,2,1,0:T(8,128)} %bitcast.13, f32[1]{0:T(128)S(6)} %copy.17.wave_ref, s32[1,2,32]{2,1,0:T(2,128)} %bitcast.18, s32[4,8]{1,0:T(4,128)} %brick_ref.1), custom_call_target="tpu_custom_call" | custom-call | tf_op jit(solution)/shard_map/pallas_call | solution.py:435
  52.6 1.8 %shard_map.104 = (f32[192,128]{1,0:T(8,128)}, f32[192,128]{1,0:T(8,128)}, f32[192,128]{1,0:T(8,128)}) custom-call(f32[128,128]{1,0:T(8,128)} %shard_map.103.desc_ref, f32[192,128]{1,0:T(8,128)} %bitcast.12, f32[192,128]{1,0:T(8,128)} %bitcast.16, f32[192,128]{1,0:T(8,128)} %bitcast.17, f32[64,128]{1,0:T(8,128)} %bitcast.15), custom_call_target="tpu_custom_call" | custom-call | tf_op jit(solution)/shard_map/pallas_call | solution.py:477

commit v3 on v2

--- a/solution.py
+++ b/solution.py
@@ -27,7 +27,19 @@
 adam_eps = 1e-08
 
 MESH = pl.DeviceIdType.MESH
-HIGHEST = lax.Precision.HIGHEST
+
+
+def picked(which, x):
+    high = x.astype(jnp.bfloat16)
+    rest = x - high.astype(jnp.float32)
+    middle = rest.astype(jnp.bfloat16)
+    low = (rest - middle.astype(jnp.float32)).astype(jnp.bfloat16)
+    which = which.astype(jnp.bfloat16)
+    return jnp.dot(
+        jnp.concatenate([which, which, which], 1),
+        jnp.concatenate([high, middle, low], 0),
+        preferred_element_type=jnp.float32,
+    )
 
 
 def quarters(shape=(K, LANES)):
@@ -93,10 +105,13 @@
     mod_hbm,
     fib_hbm,
     meas_hbm,
+    wave_hbm,
+    send_hbm,
+    brick_hbm,
+    out_ref,
     wave_ref,
     send_ref,
     brick_ref,
-    out_ref,
     mod_v,
     fib_v,
     val_v,
@@ -104,6 +119,7 @@
     in1,
     cnt_out,
     cnt_in,
+    names_v,
     ent,
     in2,
     meas_v,
@@ -123,15 +139,20 @@
     out4,
     in4,
     own5,
-    in5,
     local_sem,
     send_sem,
     recv_sem,
 ):
     subs = SUBZ // group
     slots = zones * CAP
-    me_z = lax.axis_index("zone")
+    heights = zones // 2
+    me_zone = lax.axis_index("zone")
+    me_z = lax.div(me_zone, 2)
+    me_x = lax.rem(me_zone, 2)
     me_f = lax.axis_index("freq")
+    me_t = me_x * freqs + me_f
+    level = 2 * freqs
+    block = 2 * CAP
     plane = lax.rem(me_f, 2)
     row = lax.div(me_f, 2)
     member = lax.rem(me_f, group)
@@ -144,22 +165,36 @@
     )
     barrier = pltpu.get_barrier_semaphore()
 
+    def far_first(me, i, n):
+        k = lax.div(i, 2)
+        return lax.rem(me + n + n // 2 + jnp.where(lax.rem(i, 2) == 0, k, -k), n)
+
+    def at_height(z):
+        return (z * 2 + me_x, me_f)
+
+    def at_place(t):
+        return (me_z * 2 + lax.div(t, freqs), lax.rem(t, freqs))
+
     def greet_z(i, c):
-        pl.semaphore_signal(
-            barrier, inc=1, device_id=(lax.rem(me_z + zones + zones // 2 + jnp.where(lax.rem(i, 2) == 0, lax.div(i, 2), -lax.div(i, 2)), zones), me_f), device_id_type=MESH
-        )
+        peer = at_height(far_first(me_z, i, heights))
+        pl.semaphore_signal(barrier, inc=1, device_id=peer, device_id_type=MESH)
         return c
 
-    def greet_f(i, c):
-        pl.semaphore_signal(
-            barrier, inc=1, device_id=(me_z, lax.rem(me_f + i, freqs)), device_id_type=MESH
-        )
+    def greet_near(i, c):
+        peer = at_place(far_first(me_t, i, level))
+        pl.semaphore_signal(barrier, inc=1, device_id=peer, device_id_type=MESH)
         return c
 
-    lax.fori_loop(1, zones, greet_z, 0)
-    lax.fori_loop(1, freqs, greet_f, 0)
+    lax.fori_loop(1, heights, greet_z, 0)
+    lax.fori_loop(1, level, greet_near, 0)
+    load_send = pltpu.make_async_copy(send_hbm, send_ref, local_sem.at[3])
+    load_brick = pltpu.make_async_copy(brick_hbm, brick_ref, local_sem.at[4])
+    load_wave = pltpu.make_async_copy(wave_hbm, wave_ref, local_sem.at[5])
+    load_send.start()
     load_mod.start()
     load_fib.start()
+    load_brick.start()
+    load_wave.start()
     load_meas.start()
 
     load_mod.wait()
@@ -170,43 +205,37 @@
     fibre = fib_v[pl.ds(row, NB, stride=YH), :]
     shear = first + (second - first) * fibre * fibre
     val_v[...] = jnp.where(plane == 0, shear, damp)
+    load_send.wait()
     for d in range(zones):
         for c in range(CAP):
             pick = jnp.maximum(send_ref[0, c, d], 0)
             out1[d * CAP + c : d * CAP + c + 1, :] = val_v[pl.ds(pick, 1), :]
 
-    pl.semaphore_wait(barrier, zones + freqs - 2)
-
-    def over_z(src, dst, n):
+    pl.semaphore_wait(barrier, heights + level - 2)
+
+    def send_all(me, count, device, src, dst, n):
         def body(i, c):
-            k = lax.div(i, 2)
-            peer = lax.rem(me_z + zones + zones // 2 + jnp.where(lax.rem(i, 2) == 0, k, -k), zones)
+            peer = far_first(me, i, count)
             pltpu.make_async_remote_copy(
                 src_ref=src(peer),
                 dst_ref=dst,
                 send_sem=send_sem.at[n],
                 recv_sem=recv_sem.at[n],
-                device_id=(peer, me_f),
+                device_id=device(peer),
                 device_id_type=MESH,
             ).start()
             return c
 
-        lax.fori_loop(1, zones, body, 0)
+        lax.fori_loop(1, count, body, 0)
+
+    def over_z(src, dst, n):
+        send_all(me_z, heights, at_height, src, dst, n)
+
+    def over_near(src, dst, n):
+        send_all(me_t, level, at_place, src, dst, n)
 
     def over_f(src, dst, n):
-        def body(i, c):
-            peer = lax.rem(me_f + i, freqs)
-            pltpu.make_async_remote_copy(
-                src_ref=src(peer),
-                dst_ref=dst,
-                send_sem=send_sem.at[n],
-                recv_sem=recv_sem.at[n],
-                device_id=(me_z, peer),
-                device_id_type=MESH,
-            ).start()
-            return c
-
-        lax.fori_loop(1, freqs, body, 0)
+        send_all(me_f, freqs, lambda f: (me_zone, f), src, dst, n)
 
     def arrived(ref, n):
         pltpu.make_async_copy(ref, ref, recv_sem.at[n]).wait()
@@ -214,10 +243,16 @@
     def sent(ref, n):
         pltpu.make_async_copy(ref, ref, send_sem.at[n]).wait()
 
-    mine2 = pl.ds(me_z * CAP, CAP)
-    over_z(lambda p: out1.at[pl.ds(p * CAP, CAP)], in1.at[mine2], 0)
-    in1[mine2, :] = out1[mine2, :]
-
+    mine4 = pl.ds(pl.multiple_of(me_z * block, block), block)
+    others4 = pl.ds(0, (heights - 1) * block)
+
+    def block_of(ref):
+        return lambda z: ref.at[pl.ds(pl.multiple_of(z * block, block), block)]
+
+    over_z(block_of(out1), in1.at[mine4], 0)
+    in1[mine4, :] = out1[mine4, :]
+
+    load_wave.wait()
     wave_v[member] = jnp.full((8, LANES), wave_ref[0], jnp.float32)
 
     def share(i, c):
@@ -227,7 +262,7 @@
             dst_ref=meas_v.at[member],
             send_sem=send_sem.at[1],
             recv_sem=recv_sem.at[1],
-            device_id=(me_z, base + j),
+            device_id=(me_zone, base + j),
             device_id_type=MESH,
         ).start()
         pltpu.make_async_remote_copy(
@@ -235,7 +270,7 @@
             dst_ref=wave_v.at[member],
             send_sem=send_sem.at[2],
             recv_sem=recv_sem.at[2],
-            device_id=(me_z, base + j),
+            device_id=(me_zone, base + j),
             device_id_type=MESH,
         ).start()
         return c
@@ -244,24 +279,42 @@
         lax.fori_loop(1, group, share, 0)
 
     entries = SUBZ * K
-    lane_e = lax.broadcasted_iota(jnp.int32, (1, entries), 1)
-    names = jnp.zeros((1, entries), jnp.int32)
+    load_brick.wait()
+    lane = lax.broadcasted_iota(jnp.int32, (8, LANES), 1)
+    names = jnp.full((8, LANES), -1, jnp.int32)
     for e in range(entries):
-        names = jnp.where(lane_e == e, brick_ref[e // K, e % K], names)
-    named = (lax.broadcasted_iota(jnp.int32, (slots, entries), 0) == names).astype(jnp.float32)
+        names = jnp.where(lane == e, brick_ref[e // K, e % K], names)
+    names_v[me_x] = names
+    swap = pltpu.make_async_remote_copy(
+        src_ref=names_v.at[me_x],
+        dst_ref=names_v.at[me_x],
+        send_sem=send_sem.at[8],
+        recv_sem=recv_sem.at[8],
+        device_id=(me_z * 2 + 1 - me_x, me_f),
+        device_id_type=MESH,
+    )
+    swap.start()
+    swap.wait_recv()
+    both = jnp.where(lane < entries, names_v[0], pltpu.roll(names_v[1], entries, 1))[:1]
+    half = lane[:1] // entries
+    slot = (both // 4) * 4 + half * CAP + both % 2
+    ours = (both // 2) % 2 == me_x
+    slot = jnp.where((half < 2) & ours, slot, -1)
+    named = (lax.broadcasted_iota(jnp.int32, (slots, LANES), 0) == slot).astype(jnp.float32)
+    namers = jnp.transpose(named)[: 2 * entries]
     cnt_out[...] = jnp.broadcast_to(jnp.sum(named, 1, keepdims=True), (slots, LANES))
-    over_z(lambda p: cnt_out.at[pl.ds(p * CAP, CAP)], cnt_in.at[mine2], 3)
-    cnt_in[mine2, :] = cnt_out[mine2, :]
-
-    arrived(in1.at[pl.ds(0, (zones - 1) * CAP)], 0)
-    for e in range(entries):
-        ent[e // K, e % K : e % K + 1, :] = in1[pl.ds(brick_ref[e // K, e % K], 1), :]
-    over_f(
-        lambda p: ent.at[pl.ds(lax.rem(p, group) * subs, subs)],
-        in2.at[me_f],
+    over_z(block_of(cnt_out), cnt_in.at[mine4], 3)
+    cnt_in[mine4, :] = cnt_out[mine4, :]
+    named = named[:, : 2 * entries]
+
+    arrived(in1.at[others4], 0)
+    ent[...] = picked(namers, in1[...]).reshape(2 * SUBZ, K, LANES)
+    over_near(
+        lambda t: ent.at[lax.div(t, freqs) * SUBZ + lax.rem(t, group)],
+        in2.at[me_t],
         4,
     )
-    in2[me_f] = ent[pl.ds(member * subs, subs)]
+    in2[me_t] = ent[me_x * SUBZ + member]
 
     load_meas.wait()
     if group > 1:
@@ -294,10 +347,12 @@
             held = jnp.where(lane_s == d * CAP + c, send_ref[0, c, d], held)
     holds = (lax.broadcasted_iota(jnp.int32, (NB, slots), 0) == held).astype(jnp.float32)
 
-    arrived(in2.at[pl.ds(0, freqs - 1)], 4)
+    arrived(in2.at[pl.ds(0, level - 1)], 4)
 
     for y in range(YH):
-        for q, (shear, damp) in enumerate(zip(spread(in2[2 * y, 0]), spread(in2[2 * y + 1, 0]))):
+        shears = spread(in2[2 * y] + in2[freqs + 2 * y])
+        damps = spread(in2[2 * y + 1] + in2[freqs + 2 * y + 1])
+        for q, (shear, damp) in enumerate(zip(shears, damps)):
             inv = 1.0 / (6.0 * shear + wave)
             a = relax_rate * shear * inv
             a_v[4 * y + q] = a
@@ -349,8 +404,8 @@
                 by_damp = a * by_b
                 for h in range(STEP // 4):
                     n = y // 4 + h
-                    gout[2 * n, 0] = folded([by_shear[4 * h + q] for q in range(4)])
-                    gout[2 * n + 1, 0] = folded([by_damp[4 * h + q] for q in range(4)])
+                    gout[2 * n] = folded([by_shear[4 * h + q] for q in range(4)])
+                    gout[2 * n + 1] = folded([by_damp[4 * h + q] for q in range(4)])
         if t:
             for y in range(0, BY, STEP):
                 rows = slice(y, y + STEP)
@@ -358,40 +413,42 @@
                 lam = lam_v[:, rows]
                 lam_v[:, rows] = 1.25 * lam - 6.0 * (push + a_v[rows] * lam) + near
 
-    over_f(lambda p: gout.at[p], in3.at[me_f], 5)
-    in3[me_f] = gout[me_f]
-    arrived(in3.at[pl.ds(0, freqs - 1)], 5)
+    over_near(lambda t: gout.at[lax.rem(t, freqs)], in3.at[me_t], 5)
+    in3[me_t] = gout[me_f]
+    arrived(in3.at[pl.ds(0, level - 1)], 5)
     parts = []
-    for j in range(group):
-        total = in3[j]
-        for m in range(1, freqs // group):
-            total = total + in3[m * group + j]
-        parts.append(total.reshape(subs * K, LANES))
-    grads = jnp.concatenate(parts, 0)
-    out4[...] = jnp.dot(named, grads, precision=HIGHEST, preferred_element_type=jnp.float32)
-    over_z(lambda p: out4.at[pl.ds(p * CAP, CAP)], in4.at[mine2], 6)
-    in4[mine2, :] = out4[mine2, :]
-    arrived(cnt_in.at[pl.ds(0, (zones - 1) * CAP)], 3)
-    uses = jnp.dot(holds, cnt_in[...], precision=HIGHEST, preferred_element_type=jnp.float32)
+    for h in range(2):
+        for j in range(group):
+            total = in3[h * freqs + j]
+            for m in range(1, freqs // group):
+                total = total + in3[h * freqs + m * group + j]
+            parts.append(total)
+    out4[...] = picked(named, jnp.concatenate(parts, 0))
+    over_z(block_of(out4), in4.at[mine4], 6)
+    in4[mine4, :] = out4[mine4, :]
+    arrived(cnt_in.at[others4], 3)
+    uses = picked(holds, cnt_in[...])
     scale = 1.0 / (freqs * jnp.maximum(uses, 1.0))
-    arrived(in4.at[pl.ds(0, (zones - 1) * CAP)], 6)
-    owned = jnp.dot(holds, in4[...], precision=HIGHEST, preferred_element_type=jnp.float32)
+    arrived(in4.at[others4], 6)
+    owned = picked(holds, in4[...])
     own5[...] = owned * scale
     mine8 = pl.ds(pl.multiple_of(me_f * NB, NB), NB)
-    over_f(lambda p: own5, in5.at[mine8], 7)
-    in5[mine8, :] = own5[...]
-    arrived(in5.at[pl.ds(0, (freqs - 1) * NB)], 7)
-    out_ref[...] = in5[...]
-
-    sent(out1.at[pl.ds(0, (zones - 1) * CAP)], 0)
+    over_f(lambda p: own5, out_ref.at[mine8], 7)
+    keep = pltpu.make_async_copy(own5, out_ref.at[mine8], local_sem.at[0])
+    keep.start()
+    arrived(out_ref.at[pl.ds(0, (freqs - 1) * NB)], 7)
+    keep.wait()
+
+    sent(out1.at[others4], 0)
     if group > 1:
         sent(meas_v.at[pl.ds(0, group - 1)], 1)
         sent(wave_v.at[pl.ds(0, group - 1)], 2)
-    sent(cnt_out.at[pl.ds(0, (zones - 1) * CAP)], 3)
-    sent(in2.at[pl.ds(0, freqs - 1)], 4)
-    sent(gout.at[pl.ds(0, freqs - 1)], 5)
-    sent(out4.at[pl.ds(0, (zones - 1) * CAP)], 6)
-    sent(in5.at[pl.ds(0, (freqs - 1) * NB)], 7)
+    sent(cnt_out.at[others4], 3)
+    swap.wait_send()
+    sent(in2.at[pl.ds(0, level - 1)], 4)
+    sent(in3.at[pl.ds(0, level - 1)], 5)
+    sent(out4.at[others4], 6)
+    sent(out_ref.at[pl.ds(0, (freqs - 1) * NB)], 7)
 
 
 def update(desc_ref, mod_ref, first_ref, second_ref, fib_ref, new_mod, new_first, new_second):
@@ -429,15 +486,17 @@
     f32 = jnp.float32
     vmem = pltpu.VMEM
     any_spec = pl.BlockSpec(memory_space=pl.ANY)
-    smem_spec = pl.BlockSpec(memory_space=pltpu.SMEM)
     vmem_spec = pl.BlockSpec(memory_space=vmem)
     plane_shape = (2, YH, K, LANES)
     descent = pl.pallas_call(
         functools.partial(exchange, zones, freqs, group),
         out_shape=jax.ShapeDtypeStruct((freqs * NB, LANES), f32),
-        in_specs=[any_spec, any_spec, any_spec, smem_spec, smem_spec, smem_spec],
-        out_specs=vmem_spec,
+        in_specs=[any_spec, any_spec, any_spec, any_spec, any_spec, any_spec],
+        out_specs=any_spec,
         scratch_shapes=[
+            pltpu.SMEM((1,), f32),
+            pltpu.SMEM((1, CAP, zones), jnp.int32),
+            pltpu.SMEM((SUBZ, K), jnp.int32),
             vmem((NB * 3 * YH, LANES), f32),
             vmem((NB * YH, LANES), f32),
             vmem((NB, LANES), f32),
@@ -445,8 +504,9 @@
             vmem((slots, LANES), f32),
             vmem((slots, LANES), f32),
             vmem((slots, LANES), f32),
-            vmem((SUBZ, K, LANES), f32),
-            vmem((freqs, subs, K, LANES), f32),
+            vmem((2, 8, LANES), jnp.int32),
+            vmem((2 * SUBZ, K, LANES), f32),
+            vmem((2 * freqs, K, LANES), f32),
             vmem((group, subs) + plane_shape, f32),
             vmem((group, 8, LANES), f32),
             vmem((SWEEPS, 2, BY + 2, K, LANES), f32),
@@ -459,15 +519,14 @@
             vmem((2, BY + 2, K, LANES), f32),
             vmem((BY, K, LANES), f32),
             vmem((BY, K, LANES), f32),
-            vmem((freqs, subs, K, LANES), f32),
-            vmem((freqs, subs, K, LANES), f32),
+            vmem((freqs, K, LANES), f32),
+            vmem((2 * freqs, K, LANES), f32),
             vmem((slots, LANES), f32),
             vmem((slots, LANES), f32),
             vmem((NB, LANES), f32),
-            vmem((freqs * NB, LANES), f32),
-            pltpu.SemaphoreType.DMA((3,)),
-            pltpu.SemaphoreType.DMA((8,)),
-            pltpu.SemaphoreType.DMA((8,)),
+            pltpu.SemaphoreType.DMA((6,)),
+            pltpu.SemaphoreType.DMA((9,)),
+            pltpu.SemaphoreType.DMA((9,)),
         ],
         compiler_params=pltpu.CompilerParams(
             collective_id=0, has_side_effects=True, vmem_limit_bytes=60 * 2**20

time: 54.7 us -> 51.7 us (0.945)
  Pallas kernels: 53.2 us -> 50.2 us
    pallas_call x1, Pallas kernels: 51.4 us -> 48.4 us  [on_device(): pl.pallas_call(functools.partial(exchange, zones, freqs, group), out_shap...]
where the time goes in v3:
time: 51.7 us; the launch traced here: 51.5 us
  Pallas kernels  50.2 us (97%)
  between operations  1.28 us (2%)
    pallas_call x1, Pallas kernels, on_device(): pl.pallas_call(functools.partial(exchange, zones, freqs, group), out_shap...  48.4 us
    pallas_call x1, Pallas kernels, on_device(): pl.pallas_call(update, out_shape=(made, made, made), in_specs=[vmem_spec]...  1.83 us

profile of v3, /device:TPU:1, one launch (start us, length us, event | category | flops | bytes accessed | tf_op | source)
XLA Modules:
  0.0 51.5 jit_solution(2592806045039454511)
XLA Ops:
  1.3 48.4 %shard_map.103.desc_ref = f32[128,128]{1,0:T(8,128)} custom-call(f32[192,128]{1,0:T(8,128)} %bitcast.11, f32[64,128]{1,0:T(8,128)} %bitcast.14, f32[4,2,8,8,128]{4,3,2,1,0:T(8,128)} %bitcast.13, f32[1]{0:T(128)S(6)} %copy.17.wave_hbm, s32[1,2,32]{2,1,0:T(2,128)} %bitcast.18, s32[4,8]{1,0:T(4,128)} %brick_hbm.1), custom_call_target="tpu_custom_call" | custom-call | tf_op jit(solution)/shard_map/pallas_call | solution.py:491
  49.7 1.8 %shard_map.104 = (f32[192,128]{1,0:T(8,128)}, f32[192,128]{1,0:T(8,128)}, f32[192,128]{1,0:T(8,128)}) custom-call(f32[128,128]{1,0:T(8,128)} %shard_map.103.desc_ref, f32[192,128]{1,0:T(8,128)} %bitcast.12, f32[192,128]{1,0:T(8,128)} %bitcast.16, f32[192,128]{1,0:T(8,128)} %bitcast.17, f32[64,128]{1,0:T(8,128)} %bitcast.15), custom_call_target="tpu_custom_call" | custom-call | tf_op jit(solution)/shard_map/pallas_call | solution.py:536

commit v4 on v3

--- a/solution.py
+++ b/solution.py
@@ -16,7 +16,7 @@
 LANES = 128
 SWEEPS = 6
 BY = 32
-STEP = 8
+STEP = 16
 GROUP = 4
 
 relax_rate = 0.25
@@ -324,8 +324,9 @@
     for t in range(SWEEPS):
         field_v[t, :, 0] = jnp.zeros((2, K, LANES), jnp.float32)
         field_v[t, :, BY + 1] = jnp.zeros((2, K, LANES), jnp.float32)
-    push_v[:, 0] = jnp.zeros((2, K, LANES), jnp.float32)
-    push_v[:, BY + 1] = jnp.zeros((2, K, LANES), jnp.float32)
+    for n in range(2):
+        push_v[n, :, 0] = jnp.zeros((2, K, LANES), jnp.float32)
+        push_v[n, :, BY + 1] = jnp.zeros((2, K, LANES), jnp.float32)
     for p in range(2):
         for y in range(YH):
             for q, tile in enumerate(transposed([meas_v[g, 0, p, y] for g in range(group)])):
@@ -385,20 +386,26 @@
     for t in reversed(range(SWEEPS)):
         for y in range(0, BY, STEP):
             rows = slice(y, y + STEP)
+            inner = slice(y + 1, y + 1 + STEP)
+            a, b = a_v[rows], b_v[rows]
             lam = lam_v[:, rows]
+            if t < SWEEPS - 1:
+                push, near = beside_sum(push_v.at[(t + 1) % 2], y)
+                lam = 1.25 * lam - 6.0 * (push + a * lam) + near
+                if t:
+                    lam_v[:, rows] = lam
             w = sten_v[t, :, rows]
-            v = w - 6.0 * field_v[t, :, y + 1 : y + 1 + STEP]
+            v = w - 6.0 * field_v[t, :, inner]
             by_a = lam[0] * v[0] + lam[1] * v[1]
             by_b = lam[1] * w[0] - lam[0] * w[1]
             if t < SWEEPS - 1:
                 by_a += by_a_v[rows]
                 by_b += by_b_v[rows]
-            a, b = a_v[rows], b_v[rows]
             if t:
                 by_a_v[rows] = by_a
                 by_b_v[rows] = by_b
-                push_v[0, y + 1 : y + 1 + STEP] = a * lam[0] + b * lam[1]
-                push_v[1, y + 1 : y + 1 + STEP] = a * lam[1] - b * lam[0]
+                push_v[t % 2, 0, inner] = a * lam[0] + b * lam[1]
+                push_v[t % 2, 1, inner] = a * lam[1] - b * lam[0]
             else:
                 by_shear = (by_a + damp_v[rows] * by_b) * slope_v[rows]
                 by_damp = a * by_b
@@ -406,12 +413,6 @@
                     n = y // 4 + h
                     gout[2 * n] = folded([by_shear[4 * h + q] for q in range(4)])
                     gout[2 * n + 1] = folded([by_damp[4 * h + q] for q in range(4)])
-        if t:
-            for y in range(0, BY, STEP):
-                rows = slice(y, y + STEP)
-                push, near = beside_sum(push_v, y)
-                lam = lam_v[:, rows]
-                lam_v[:, rows] = 1.25 * lam - 6.0 * (push + a_v[rows] * lam) + near
 
     over_near(lambda t: gout.at[lax.rem(t, freqs)], in3.at[me_t], 5)
     in3[me_t] = gout[me_f]
@@ -516,7 +517,7 @@
             vmem((BY, K, LANES), f32),
             vmem((BY, K, LANES), f32),
             vmem((2, BY, K, LANES), f32),
-            vmem((2, BY + 2, K, LANES), f32),
+            vmem((2, 2, BY + 2, K, LANES), f32),
             vmem((BY, K, LANES), f32),
             vmem((BY, K, LANES), f32),
             vmem((freqs, K, LANES), f32),

time: 51.7 us -> 52 us (level)
  no operation moved by 1% of the time
where the time goes in v4:
time: 52 us; the launch traced here: 51.8 us
  Pallas kernels  50.5 us (97%)
  between operations  1.28 us (2%)
    pallas_call x1, Pallas kernels, on_device(): pl.pallas_call(functools.partial(exchange, zones, freqs, group), out_shap...  48.7 us
    pallas_call x1, Pallas kernels, on_device(): pl.pallas_call(update, out_shape=(made, made, made), in_specs=[vmem_spec]...  1.83 us

profile of v4, /device:TPU:1, one launch (start us, length us, event | category | flops | bytes accessed | tf_op | source)
XLA Modules:
  0.0 51.8 jit_solution(7786291688030856907)
XLA Ops:
  1.3 48.7 %shard_map.103.desc_ref = f32[128,128]{1,0:T(8,128)} custom-call(f32[192,128]{1,0:T(8,128)} %bitcast.11, f32[64,128]{1,0:T(8,128)} %bitcast.14, f32[4,2,8,8,128]{4,3,2,1,0:T(8,128)} %bitcast.13, f32[1]{0:T(128)S(6)} %copy.17.wave_hbm, s32[1,2,32]{2,1,0:T(2,128)} %bitcast.18, s32[4,8]{1,0:T(4,128)} %brick_hbm.1), custom_call_target="tpu_custom_call" | custom-call | tf_op jit(solution)/shard_map/pallas_call | solution.py:492
  50.0 1.8 %shard_map.104 = (f32[192,128]{1,0:T(8,128)}, f32[192,128]{1,0:T(8,128)}, f32[192,128]{1,0:T(8,128)}) custom-call(f32[128,128]{1,0:T(8,128)} %shard_map.103.desc_ref, f32[192,128]{1,0:T(8,128)} %bitcast.12, f32[192,128]{1,0:T(8,128)} %bitcast.16, f32[192,128]{1,0:T(8,128)} %bitcast.17, f32[64,128]{1,0:T(8,128)} %bitcast.15), custom_call_target="tpu_custom_call" | custom-call | tf_op jit(solution)/shard_map/pallas_call | solution.py:537
